TPU v7x, 128 devices: a whole 4x4x4 slice. The times are simulated.
128 devices in a mesh: gy: 32 (over z, y, x_lo), gz: 4 (over x_hi, core).
Axes of the slice: x: 4 (x_hi: 2, x_lo: 2; x = x_hi * 2 + x_lo), y: 4, z: 4, core: 2. Of those that a mesh axis runs over, the one named last changes fastest.
Arguments:
- estimate: float32 [128, 512, 512], P('gz', 'gy'), may hold values from 0.5 to 2
- observed: float32 [4, 128, 512, 512], P(None, 'gz', 'gy'), may hold values from 0.25 to 4
- tile_order: int32 [4, 32], replicated, may hold values from 0 to 31, each once within a row
- lateral_taps: float32 [4, 2, 9], replicated, may hold values from 0.02 to 0.2
- axial_taps: float32 [4, 33], replicated, may hold values from 0.01 to 0.06
Outputs:
- updated: float32 [128, 512, 512], P('gz', 'gy')
Inputs may be any that keep to these rules, and one draw needn't show every extreme that they name: `tile_order`: each row is a permutation of the 32 tiles.
All inputs are finite; a program needn't handle non-finite values.
Results may differ from a plain program's by a relative error of at most 0.00005.
Values sent between devices are 32-bit elements; how exact they have to be, the bound alone decides.
A program may use at most 256 MiB of HBM per device.

v0:
```python
import functools

import jax
import jax.numpy as jnp
from jax import lax
from jax.experimental import pallas as pl
from jax.experimental.pallas import tpu as pltpu
from jax.sharding import PartitionSpec as P

MESH = pl.DeviceIdType.MESH
F32 = jnp.float32
BF16 = jnp.bfloat16

NV = 4
TAX = 33
TLAT = 9
PL = 32
RW = 16
W = 512
PEERS = 32
SLABS = 4
HZ = TAX // 2
HY = TLAT // 2
PE = PL + 2 * HZ
RE = RW + 2 * HY
ZG = PL // 8
CC = W // 128


def split(value):
    high = value.astype(BF16)
    return high, (value - high.astype(F32)).astype(BF16)


def dot(a, b):
    return jnp.dot(a, b, preferred_element_type=F32)


def dot_nt(a, b):
    return lax.dot_general(a, b, (((1,), (1,)), ((), ())), preferred_element_type=F32)


def swap_chunks(vals, chunk):
    span = vals[0].shape[-1]
    which = lax.broadcasted_iota(jnp.int32, vals[0].shape, vals[0].ndim - 1) // chunk
    for b in (4, 2, 1):
        low = (which & b) == 0
        new = list(vals)
        for k in range(8):
            if k & b:
                continue
            new[k] = jnp.where(low, vals[k], pltpu.roll(vals[k | b], b * chunk, 1))
            new[k | b] = jnp.where(low, pltpu.roll(vals[k], span - b * chunk, 1), vals[k | b])
        vals = new
    return vals


def kernel(
    est_hbm, obs_hbm, order, lat, axial, out_ref,
    est_v, obs_v, snd, rcv, ext, axb, lh, ll, bl, qh, ql, rh, rl, tt, acat, at_h, at_l, gb, zr, yr,
    lsem, a_send, a_recv, y_send, y_recv, z_send, z_recv, zb_send, zb_recv, yb_send, yb_recv,
):
    gy = lax.axis_index("gy")
    gz = lax.axis_index("gz")
    cz, cy, cx = gy // 8, (gy // 2) % 4, gy % 2

    est_in = [
        pltpu.make_async_copy(est_hbm.at[:, c * 128 : (c + 1) * 128], est_v.at[c], lsem.at[NV + c])
        for c in range(CC)
    ]
    for copy in est_in:
        copy.start()
    for v in range(NV):
        pltpu.make_async_copy(obs_hbm.at[v], obs_v.at[v], lsem.at[v]).start()

    def peer(k):
        return ((cz + k // 8) % 4) * 8 + ((cy + (k // 2) % 4) % 4) * 2 + (cx + k % 2) % 2

    bar = pltpu.get_barrier_semaphore()

    def greet(k, carry):
        pl.semaphore_signal(bar, inc=1, device_id=(peer(k), gz), device_id_type=MESH)
        return carry

    lax.fori_loop(1, PEERS, greet, 0)
    up_z, dn_z = (gz + 1) % SLABS, (gz + SLABS - 1) % SLABS
    up_y, dn_y = (gy + 1) % PEERS, (gy + PEERS - 1) % PEERS
    for other in (up_z, dn_z):
        pl.semaphore_signal(bar, inc=1, device_id=(gy, other), device_id_type=MESH)

    for c, copy in enumerate(est_in):
        copy.wait()
        for y in range(RW):
            ext[HY + y, HZ : HZ + PL, c * 128 : (c + 1) * 128] = est_v[c, pl.ds(y, PL, stride=RW), :]

    @pl.when(gy == 0)
    def _():
        ext[0:HY, HZ : HZ + PL, :] = jnp.zeros((HY, PL, W), F32)

    @pl.when(gy == PEERS - 1)
    def _():
        ext[HY + RW : RE, HZ : HZ + PL, :] = jnp.zeros((HY, PL, W), F32)

    @pl.when(gz == 0)
    def _():
        ext[:, 0:HZ, :] = jnp.zeros((RE, HZ, W), F32)

    @pl.when(gz == SLABS - 1)
    def _():
        ext[:, HZ + PL : PE, :] = jnp.zeros((RE, HZ, W), F32)

    pl.semaphore_wait(bar, PEERS - 1 + 2)

    def y_copy(side):
        src = (slice(HY, 2 * HY), slice(RW, RW + HY))[side]
        dst = (slice(HY + RW, RE), slice(0, HY))[side]
        return pltpu.make_async_remote_copy(
            ext.at[src, HZ : HZ + PL], ext.at[dst, HZ : HZ + PL], y_send.at[side], y_recv.at[side],
            device_id=((dn_y, up_y)[side], gz), device_id_type=MESH,
        )

    def z_copy(side, part):
        rows = (slice(HY, HY + RW), slice(0, HY), slice(HY + RW, RE))[part]
        src = (slice(HZ, 2 * HZ), slice(PL, PL + HZ))[side]
        dst = (slice(HZ + PL, PE), slice(0, HZ))[side]
        return pltpu.make_async_remote_copy(
            ext.at[rows, src], ext.at[rows, dst], z_send.at[side, part], z_recv.at[side, part],
            device_id=(gy, (dn_z, up_z)[side]), device_id_type=MESH,
        )

    has_y = (gy > 0, gy < PEERS - 1)
    has_z = (gz > 0, gz < SLABS - 1)
    for side in range(2):

        @pl.when(has_y[side])
        def _():
            y_copy(side).start()

        @pl.when(has_z[side])
        def _():
            z_copy(side, 0).start()

    def send_view(v, carry):
        pltpu.make_async_copy(obs_hbm.at[v], obs_v.at[v], lsem.at[v]).wait()
        for g in range(ZG):
            for c in range(4):
                t = obs_v[v, g * 128 : (g + 1) * 128, c * 128 : (c + 1) * 128].T
                for d in range(8):
                    snd[v, c * 8 + d, g] = t[d * RW : (d + 1) * RW, :]
        rcv[v, gy] = snd[v, gy]

        def push(k, inner):
            to = peer(k)
            pltpu.make_async_remote_copy(
                snd.at[v, to], rcv.at[v, gy], a_send.at[v], a_recv.at[v],
                device_id=(to, gz), device_id_type=MESH,
            ).start()
            return inner

        lax.fori_loop(1, PEERS, push, 0)
        return carry

    lax.fori_loop(0, NV, send_view, 0)

    i0 = lax.broadcasted_iota(jnp.int32, (PL, PE), 0)
    i1 = lax.broadcasted_iota(jnp.int32, (PL, PE), 1)
    for v in range(NV):
        am = jnp.zeros((PL, PE), F32)
        for k in range(TAX):
            am = jnp.where(i1 - i0 == k, axial[v, k], am)
        high, low = split(am)
        acat[v * PL : (v + 1) * PL, :] = jnp.concatenate([high, high, low], axis=1)
    lane = lax.broadcasted_iota(jnp.int32, (1, NV * PL), 1)
    j0 = lax.broadcasted_iota(jnp.int32, (PE, NV * PL), 0)
    j1 = lax.broadcasted_iota(jnp.int32, (PE, NV * PL), 1) % PL
    am = jnp.zeros((PE, NV * PL), F32)
    for k in range(TAX):
        tap = jnp.zeros((1, NV * PL), F32)
        for v in range(NV):
            tap = jnp.where(lane // PL == v, axial[v, k], tap)
        am = jnp.where(j0 - j1 == k, tap, am)
    high, low = split(am)
    at_h[...] = jnp.concatenate([high, high], axis=1)
    at_l[...] = low

    def build(v, carry):
        col = lax.broadcasted_iota(jnp.int32, (1, W), 1)
        at = col % RW
        for s in range(PEERS):
            at = jnp.where(col // RW == s, at + order[v, s] * RW, at)
        for b in range(W // 64):
            d = lax.broadcasted_iota(jnp.int32, (64, W), 0) + (b * 64 + HY) - at
            q = jnp.zeros((64, W), F32)
            for i in range(TLAT):
                q = jnp.where(d == i, lat[v, 1, i], q)
            high, low = split(q)
            qh[v, b * 64 : (b + 1) * 64, :] = high
            ql[v, b * 64 : (b + 1) * 64, :] = low
        return carry

    lax.fori_loop(0, NV, build, 0)

    for side in range(2):

        @pl.when(has_y[1 - side])
        def _():
            y_copy(side).wait_recv()

    for side in range(2):

        @pl.when(has_z[side])
        def _():
            z_copy(side, 1).start()
            z_copy(side, 2).start()

    for side in range(2):

        @pl.when(has_z[1 - side])
        def _():
            for part in range(3):
                z_copy(side, part).wait_recv()

    def axial_row(y, carry):
        high, low = split(ext[y])
        axb[y] = dot(acat[...], jnp.concatenate([high, low, high], axis=0))
        return carry

    lax.fori_loop(0, RE, axial_row, 0)

    def row_tile(t, carry):
        v = t // 2
        taps = [lat[v, 0, j] for j in range(TLAT)]
        at = pl.multiple_of(t * 16, 16)
        m = pl.multiple_of((t % 2) * 16, 16)
        for c in range(W // 128):
            cols = slice(c * 128, (c + 1) * 128)
            rows = [axb[y, pl.ds(at, 16), cols] for y in range(RE)]
            for y in range(RW):
                acc = taps[0] * rows[y]
                for j in range(1, TLAT):
                    acc = acc + taps[j] * rows[y + j]
                high, low = split(acc)
                lh[v, pl.ds(y * PL + m, 16), cols] = high
                ll[v, pl.ds(y * PL + m, 16), cols] = low
        return carry

    lax.fori_loop(0, NV * 2, row_tile, 0)

    def col_view(v, carry):
        for n in range(2):
            cols = slice(n * 256, (n + 1) * 256)
            res = dot(lh[v], qh[v, :, cols]) + dot(ll[v], qh[v, :, cols]) + dot(lh[v], ql[v, :, cols])
            bl[v, 2 * n] = res[:, :128]
            bl[v, 2 * n + 1] = res[:, 128:]
        return carry

    lax.fori_loop(0, NV, col_view, 0)

    def back_view(v, carry):
        pltpu.make_async_copy(
            rcv.at[v, pl.ds(0, PEERS - 1)], rcv.at[v, pl.ds(0, PEERS - 1)], a_recv.at[v]
        ).wait()

        def group(g, inner):
            for s in range(PEERS // 8):
                cols = slice(s * 128, (s + 1) * 128)
                vals = swap_chunks([rcv[v, s * 8 + k, g] for k in range(8)], RW)
                for z in range(8):
                    den = bl[v, s, pl.ds(g * 8 + z, RW, stride=PL), :]
                    high, low = split(vals[z] / den)
                    at = pl.multiple_of(g * 128 + z * 16, 16)
                    rh[pl.ds(at, 16), cols] = high
                    rl[pl.ds(at, 16), cols] = low
            return inner

        lax.fori_loop(0, ZG, group, 0)
        for n in range(2):
            rows = slice(n * 256, (n + 1) * 256)
            res = dot_nt(rh[...], qh[v, rows, :]) + dot_nt(rl[...], qh[v, rows, :]) + dot_nt(rh[...], ql[v, rows, :])
            bl[v, 2 * n] = res[:, :128]
            bl[v, 2 * n + 1] = res[:, 128:]
        taps = [lat[v, 0, j] for j in range(TLAT)]

        def spread(h, inner):
            for c in range(W // 128):
                cols = slice(c * 128, (c + 1) * 128)
                rows = [bl[v, c, pl.ds(h * 256 + y, 16, stride=RW), :] for y in range(RW)]
                for y in range(RE):
                    acc = None
                    for j in range(TLAT):
                        if 0 <= y - j < RW:
                            term = taps[j] * rows[y - j]
                            acc = term if acc is None else acc + term
                    high, low = split(acc)
                    at = pl.multiple_of(v * PL + h * 16, 16)
                    tt[y, pl.ds(at, 16), cols] = high
                    tt[y, pl.ds(NV * PL + at, 16), cols] = low
            return inner

        lax.fori_loop(0, 2, spread, 0)
        return carry

    lax.fori_loop(0, NV, back_view, 0)

    def axial_back(y, carry):
        gb[y] = dot(at_h[...], tt[y]) + dot(at_l[...], tt[y, 0 : NV * PL])
        return carry

    lax.fori_loop(0, RE, axial_back, 0)

    def zb_copy(side):
        src = (slice(0, HZ), slice(HZ + PL, PE))[side]
        return pltpu.make_async_remote_copy(
            gb.at[:, src], zr.at[side], zb_send.at[side], zb_recv.at[side],
            device_id=(gy, (dn_z, up_z)[side]), device_id_type=MESH,
        )

    for side in range(2):

        @pl.when(has_z[side])
        def _():
            zb_copy(side).start()

    for side in range(2):

        @pl.when(has_z[1 - side])
        def _():
            zb_copy(side).wait_recv()
            at = (slice(PL, PL + HZ), slice(HZ, 2 * HZ))[side]

            def add(y, carry):
                gb[y, at] = gb[y, at] + zr[side, y]
                return carry

            lax.fori_loop(0, RE, add, 0)

    def yb_copy(side):
        src = (slice(0, HY), slice(HY + RW, RE))[side]
        return pltpu.make_async_remote_copy(
            gb.at[src, HZ : HZ + PL], yr.at[side], yb_send.at[side], yb_recv.at[side],
            device_id=((dn_y, up_y)[side], gz), device_id_type=MESH,
        )

    for side in range(2):

        @pl.when(has_y[side])
        def _():
            yb_copy(side).start()

    for side in range(2):

        @pl.when(has_y[1 - side])
        def _():
            yb_copy(side).wait_recv()
            base = (RW, HY)[side]
            for y in range(HY):
                gb[base + y, HZ : HZ + PL] = gb[base + y, HZ : HZ + PL] + yr[side, y]

    outs = []
    for c in range(CC):
        cols = slice(c * 128, (c + 1) * 128)
        for y in range(RW):
            est_v[c, pl.ds(y, PL, stride=RW), :] = ext[HY + y, HZ : HZ + PL, cols] * (
                gb[HY + y, HZ : HZ + PL, cols] * (1.0 / NV)
            )
        outs.append(pltpu.make_async_copy(est_v.at[c], out_ref.at[:, cols], lsem.at[NV + c]))
        outs[-1].start()
    for copy in outs:
        copy.wait()

    for side in range(2):

        @pl.when(has_y[side])
        def _():
            y_copy(side).wait_send()
            yb_copy(side).wait_send()

        @pl.when(has_z[side])
        def _():
            for part in range(3):
                z_copy(side, part).wait_send()
            zb_copy(side).wait_send()

    for v in range(NV):
        pltpu.make_async_copy(
            snd.at[v, pl.ds(0, PEERS - 1)], snd.at[v, pl.ds(0, PEERS - 1)], a_send.at[v]
        ).wait()


def local(estimate, observed, tile_order, lateral_taps, axial_taps):
    rows = PL * RW
    smem = pl.BlockSpec(memory_space=pltpu.SMEM)
    hbm = pl.BlockSpec(memory_space=pl.ANY)
    dma = pltpu.SemaphoreType.DMA
    out = pl.pallas_call(
        kernel,
        out_shape=jax.ShapeDtypeStruct((rows, W), F32),
        in_specs=[hbm, hbm, smem, smem, smem],
        out_specs=hbm,
        scratch_shapes=[
            pltpu.VMEM((CC, rows, 128), F32),
            pltpu.VMEM((NV, rows, W), F32),
            pltpu.VMEM((NV, PEERS, ZG, RW, 128), F32),
            pltpu.VMEM((NV, PEERS, ZG, RW, 128), F32),
            pltpu.VMEM((RE, PE, W), F32),
            pltpu.VMEM((RE, NV * PL, W), F32),
            pltpu.VMEM((NV, rows, W), BF16),
            pltpu.VMEM((NV, rows, W), BF16),
            pltpu.VMEM((NV, CC, rows, 128), F32),
            pltpu.VMEM((NV, W, W), BF16),
            pltpu.VMEM((NV, W, W), BF16),
            pltpu.VMEM((rows, W), BF16),
            pltpu.VMEM((rows, W), BF16),
            pltpu.VMEM((RE, 2 * NV * PL, W), BF16),
            pltpu.VMEM((NV * PL, 3 * PE), BF16),
            pltpu.VMEM((PE, 2 * NV * PL), BF16),
            pltpu.VMEM((PE, NV * PL), BF16),
            pltpu.VMEM((RE, PE, W), F32),
            pltpu.VMEM((2, RE, HZ, W), F32),
            pltpu.VMEM((2, HY, PL, W), F32),
            dma((NV + CC,)),
            dma((NV,)),
            dma((NV,)),
            dma((2,)),
            dma((2,)),
            dma((2, 3)),
            dma((2, 3)),
            dma((2,)),
            dma((2,)),
            dma((2,)),
            dma((2,)),
        ],
        compiler_params=pltpu.CompilerParams(
            collective_id=0, has_side_effects=True, vmem_limit_bytes=60 << 20
        ),
    )(
        estimate.reshape(rows, W),
        observed.reshape(NV, rows, W),
        tile_order,
        lateral_taps,
        axial_taps,
    )
    return out.reshape(PL, RW, W)


def solution(mesh):
    return jax.shard_map(
        local,
        mesh=mesh,
        in_specs=(P("gz", "gy", None), P(None, "gz", "gy", None), P(), P(), P()),
        out_specs=P("gz", "gy", None),
        check_vma=False,
    )
```

profile of v0, /device:TPU:33, one launch (start us, length us, event | category | flops | bytes accessed | tf_op | source)
XLA Modules:
  0.0 135.0 jit_solution(1602906382165182199)
XLA Ops:
  0.0 132.7 %shard_map.55 = f32[512,512]{1,0:T(8,128)} custom-call(f32[512,512]{1,0:T(8,128)} %bitcast.5, f32[4,512,512]{2,1,0:T(8,128)} %bitcast.3, s32[4,32]{1,0:T(4,128)} %order.1, f32[4,2,9]{2,1,0:T(2,128)} %lat.1, f32[4,33]{1,0:T(4,128)} %axial.1), custom_call_target="tpu_custom_call" | custom-call | tf_op jit(solution)/shard_map/pallas_call | solution.py:395
  132.7 2.3 %copy.7 = f32[32,16,512]{2,1,0:T(8,128)} copy(f32[32,16,512]{2,1,0:T(8,128)} %bitcast.4) | data formatting | bytes 2097152
where the time goes:
time: 135 us
  Pallas kernels  133 us (99%)
  local copies, waits for them, and re-layouts  2.31 us (2%)
    pallas_call x1, Pallas kernels, local(): pl.pallas_call(kernel, out_shape=jax.ShapeDtypeStruct((rows, W), F32), in...  133 us

commit v1 on v0

--- a/solution.py
+++ b/solution.py
@@ -140,6 +140,20 @@
         def _():
             z_copy(side, 0).start()
 
+    def send_margins():
+        for side in range(2):
+
+            @pl.when(has_y[1 - side])
+            def _():
+                y_copy(side).wait_recv()
+
+        for side in range(2):
+
+            @pl.when(has_z[side])
+            def _():
+                z_copy(side, 1).start()
+                z_copy(side, 2).start()
+
     def send_view(v, carry):
         pltpu.make_async_copy(obs_hbm.at[v], obs_v.at[v], lsem.at[v]).wait()
         for g in range(ZG):
@@ -160,7 +174,9 @@
         lax.fori_loop(1, PEERS, push, 0)
         return carry
 
-    lax.fori_loop(0, NV, send_view, 0)
+    send_view(0, 0)
+    send_margins()
+    lax.fori_loop(1, NV, send_view, 0)
 
     i0 = lax.broadcasted_iota(jnp.int32, (PL, PE), 0)
     i1 = lax.broadcasted_iota(jnp.int32, (PL, PE), 1)
@@ -202,19 +218,6 @@
 
     for side in range(2):
 
-        @pl.when(has_y[1 - side])
-        def _():
-            y_copy(side).wait_recv()
-
-    for side in range(2):
-
-        @pl.when(has_z[side])
-        def _():
-            z_copy(side, 1).start()
-            z_copy(side, 2).start()
-
-    for side in range(2):
-
         @pl.when(has_z[1 - side])
         def _():
             for part in range(3):
@@ -225,7 +228,7 @@
         axb[y] = dot(acat[...], jnp.concatenate([high, low, high], axis=0))
         return carry
 
-    lax.fori_loop(0, RE, axial_row, 0)
+    lax.fori_loop(0, RE, axial_row, 0, unroll=4)
 
     def row_tile(t, carry):
         v = t // 2
@@ -306,7 +309,7 @@
         gb[y] = dot(at_h[...], tt[y]) + dot(at_l[...], tt[y, 0 : NV * PL])
         return carry
 
-    lax.fori_loop(0, RE, axial_back, 0)
+    lax.fori_loop(0, RE, axial_back, 0, unroll=4)
 
     def zb_copy(side):
         src = (slice(0, HZ), slice(HZ + PL, PE))[side]

time: 135 us -> 113 us (0.84)
  Pallas kernels: 133 us -> 111 us
    pallas_call x1, Pallas kernels: 133 us -> 111 us  [local(): pl.pallas_call(kernel, out_shape=jax.ShapeDtypeStruct((rows, W), F32), in...]
where the time goes in v1:
time: 113 us
  Pallas kernels  111 us (98%)
  local copies, waits for them, and re-layouts  2.31 us (2%)
    pallas_call x1, Pallas kernels, local(): pl.pallas_call(kernel, out_shape=jax.ShapeDtypeStruct((rows, W), F32), in...  111 us
    unnamed x1, local copies, waits for them, and re-layouts  2.31 us

profile of v1, /device:TPU:33, one launch (start us, length us, event | category | flops | bytes accessed | tf_op | source)
XLA Modules:
  0.0 113.0 jit_solution(17883114800553266433)
XLA Ops:
  0.0 110.7 %shard_map.55 = f32[512,512]{1,0:T(8,128)} custom-call(f32[512,512]{1,0:T(8,128)} %bitcast.5, f32[4,512,512]{2,1,0:T(8,128)} %bitcast.3, s32[4,32]{1,0:T(4,128)} %order.1, f32[4,2,9]{2,1,0:T(2,128)} %lat.1, f32[4,33]{1,0:T(4,128)} %axial.1), custom_call_target="tpu_custom_call" | custom-call | tf_op jit(solution)/shard_map/pallas_call | solution.py:398
  110.7 2.3 %copy.7 = f32[32,16,512]{2,1,0:T(8,128)} copy(f32[32,16,512]{2,1,0:T(8,128)} %bitcast.4) | data formatting | bytes 2097152

commit v2 on v1

--- a/solution.py
+++ b/solution.py
@@ -27,6 +27,12 @@
 CC = W // 128
 
 
+PLANE = (
+    (1, 0), (0, 1), (3, 0), (0, 3), (2, 1), (1, 2), (2, 3), (3, 2), (1, 1), (3, 3), (1, 3), (3, 1), (2, 0), (0, 2), (2, 2),
+)
+ORDER = ((0, 0, 1),) + tuple((dz, dy, dx) for dz, dy in PLANE for dx in (1, 0))
+
+
 def split(value):
     high = value.astype(BF16)
     return high, (value - high.astype(F32)).astype(BF16)
@@ -57,7 +63,7 @@
 
 def kernel(
     est_hbm, obs_hbm, order, lat, axial, out_ref,
-    est_v, obs_v, snd, rcv, ext, axb, lh, ll, bl, qh, ql, rh, rl, tt, acat, at_h, at_l, gb, zr, yr,
+    est_v, obs_v, snd, rcv, ext, axb, lh, ll, bl, qh, ql, rh, rl, tt, acat, adj, gb, zr, yr,
     lsem, a_send, a_recv, y_send, y_recv, z_send, z_recv, zb_send, zb_recv, yb_send, yb_recv,
 ):
     gy = lax.axis_index("gy")
@@ -73,16 +79,13 @@
     for v in range(NV):
         pltpu.make_async_copy(obs_hbm.at[v], obs_v.at[v], lsem.at[v]).start()
 
-    def peer(k):
-        return ((cz + k // 8) % 4) * 8 + ((cy + (k // 2) % 4) % 4) * 2 + (cx + k % 2) % 2
+    def peer(dz, dy, dx):
+        return ((cz + dz) % 4) * 8 + ((cy + dy) % 4) * 2 + (cx + dx) % 2
 
     bar = pltpu.get_barrier_semaphore()
 
-    def greet(k, carry):
-        pl.semaphore_signal(bar, inc=1, device_id=(peer(k), gz), device_id_type=MESH)
-        return carry
-
-    lax.fori_loop(1, PEERS, greet, 0)
+    for offset in ORDER:
+        pl.semaphore_signal(bar, inc=1, device_id=(peer(*offset), gz), device_id_type=MESH)
     up_z, dn_z = (gz + 1) % SLABS, (gz + SLABS - 1) % SLABS
     up_y, dn_y = (gy + 1) % PEERS, (gy + PEERS - 1) % PEERS
     for other in (up_z, dn_z):
@@ -163,15 +166,12 @@
                     snd[v, c * 8 + d, g] = t[d * RW : (d + 1) * RW, :]
         rcv[v, gy] = snd[v, gy]
 
-        def push(k, inner):
-            to = peer(k)
+        for offset in ORDER:
+            to = peer(*offset)
             pltpu.make_async_remote_copy(
                 snd.at[v, to], rcv.at[v, gy], a_send.at[v], a_recv.at[v],
                 device_id=(to, gz), device_id_type=MESH,
             ).start()
-            return inner
-
-        lax.fori_loop(1, PEERS, push, 0)
         return carry
 
     send_view(0, 0)
@@ -186,18 +186,14 @@
             am = jnp.where(i1 - i0 == k, axial[v, k], am)
         high, low = split(am)
         acat[v * PL : (v + 1) * PL, :] = jnp.concatenate([high, high, low], axis=1)
-    lane = lax.broadcasted_iota(jnp.int32, (1, NV * PL), 1)
-    j0 = lax.broadcasted_iota(jnp.int32, (PE, NV * PL), 0)
-    j1 = lax.broadcasted_iota(jnp.int32, (PE, NV * PL), 1) % PL
-    am = jnp.zeros((PE, NV * PL), F32)
-    for k in range(TAX):
-        tap = jnp.zeros((1, NV * PL), F32)
-        for v in range(NV):
-            tap = jnp.where(lane // PL == v, axial[v, k], tap)
-        am = jnp.where(j0 - j1 == k, tap, am)
-    high, low = split(am)
-    at_h[...] = jnp.concatenate([high, high], axis=1)
-    at_l[...] = low
+    j0 = lax.broadcasted_iota(jnp.int32, (PE, PL), 0)
+    j1 = lax.broadcasted_iota(jnp.int32, (PE, PL), 1)
+    for v in range(NV):
+        am = jnp.zeros((PE, PL), F32)
+        for k in range(TAX):
+            am = jnp.where(j0 - j1 == k, axial[v, k], am)
+        high, low = split(am)
+        adj[v] = jnp.concatenate([high, high, low], axis=1)
 
     def build(v, carry):
         col = lax.broadcasted_iota(jnp.int32, (1, W), 1)
@@ -259,7 +255,7 @@
 
     lax.fori_loop(0, NV, col_view, 0)
 
-    def back_view(v, carry):
+    def back_view(v):
         pltpu.make_async_copy(
             rcv.at[v, pl.ds(0, PEERS - 1)], rcv.at[v, pl.ds(0, PEERS - 1)], a_recv.at[v]
         ).wait()
@@ -295,47 +291,66 @@
                             term = taps[j] * rows[y - j]
                             acc = term if acc is None else acc + term
                     high, low = split(acc)
-                    at = pl.multiple_of(v * PL + h * 16, 16)
+                    at = pl.multiple_of(h * 16, 16)
                     tt[y, pl.ds(at, 16), cols] = high
-                    tt[y, pl.ds(NV * PL + at, 16), cols] = low
+                    tt[y, pl.ds(PL + at, 16), cols] = low
+                    tt[y, pl.ds(2 * PL + at, 16), cols] = high
             return inner
 
         lax.fori_loop(0, 2, spread, 0)
-        return carry
-
-    lax.fori_loop(0, NV, back_view, 0)
-
-    def axial_back(y, carry):
-        gb[y] = dot(at_h[...], tt[y]) + dot(at_l[...], tt[y, 0 : NV * PL])
-        return carry
-
-    lax.fori_loop(0, RE, axial_back, 0, unroll=4)
-
-    def zb_copy(side):
+
+    def axial_back(v, first, start, stop):
+        def row(y, carry):
+            term = dot(adj[v], tt[y])
+            gb[y] = term if first else gb[y] + term
+            return carry
+
+        lax.fori_loop(start, stop, row, 0, unroll=4)
+
+    def whole_view(v, carry):
+        back_view(v)
+        axial_back(v, False, 0, RE)
+        return carry
+
+    back_view(0)
+    axial_back(0, True, 0, RE)
+    lax.fori_loop(1, NV - 1, whole_view, 0)
+    back_view(NV - 1)
+
+    parts = ((0, HY), (HY + RW, RE), (HY, HY + RW))
+
+    def zb_copy(side, part):
         src = (slice(0, HZ), slice(HZ + PL, PE))[side]
+        rows = slice(*parts[part])
         return pltpu.make_async_remote_copy(
-            gb.at[:, src], zr.at[side], zb_send.at[side], zb_recv.at[side],
+            gb.at[rows, src], zr.at[side, rows], zb_send.at[side, part], zb_recv.at[side, part],
             device_id=(gy, (dn_z, up_z)[side]), device_id_type=MESH,
         )
 
-    for side in range(2):
-
-        @pl.when(has_z[side])
-        def _():
-            zb_copy(side).start()
-
-    for side in range(2):
-
-        @pl.when(has_z[1 - side])
-        def _():
-            zb_copy(side).wait_recv()
-            at = (slice(PL, PL + HZ), slice(HZ, 2 * HZ))[side]
-
-            def add(y, carry):
-                gb[y, at] = gb[y, at] + zr[side, y]
-                return carry
-
-            lax.fori_loop(0, RE, add, 0)
+    def zb_start(part):
+        for side in range(2):
+
+            @pl.when(has_z[side])
+            def _():
+                zb_copy(side, part).start()
+
+    def zb_add(part):
+        for side in range(2):
+
+            @pl.when(has_z[1 - side])
+            def _():
+                zb_copy(side, part).wait_recv()
+                at = (slice(PL, PL + HZ), slice(HZ, 2 * HZ))[side]
+                for y in range(*parts[part]):
+                    gb[y, at] = gb[y, at] + zr[side, y]
+
+    for part in range(2):
+        axial_back(NV - 1, False, *parts[part])
+        zb_start(part)
+    axial_back(NV - 1, False, *parts[2])
+    zb_start(2)
+    for part in range(2):
+        zb_add(part)
 
     def yb_copy(side):
         src = (slice(0, HY), slice(HY + RW, RE))[side]
@@ -350,6 +365,17 @@
         def _():
             yb_copy(side).start()
 
+    zb_add(2)
+
+    def finish(rows):
+        for c in range(CC):
+            cols = slice(c * 128, (c + 1) * 128)
+            for y in rows:
+                est_v[c, pl.ds(y, PL, stride=RW), :] = ext[HY + y, HZ : HZ + PL, cols] * (
+                    gb[HY + y, HZ : HZ + PL, cols] * (1.0 / NV)
+                )
+
+    finish(range(HY, RW - HY))
     for side in range(2):
 
         @pl.when(has_y[1 - side])
@@ -359,13 +385,10 @@
             for y in range(HY):
                 gb[base + y, HZ : HZ + PL] = gb[base + y, HZ : HZ + PL] + yr[side, y]
 
+    finish([*range(HY), *range(RW - HY, RW)])
     outs = []
     for c in range(CC):
         cols = slice(c * 128, (c + 1) * 128)
-        for y in range(RW):
-            est_v[c, pl.ds(y, PL, stride=RW), :] = ext[HY + y, HZ : HZ + PL, cols] * (
-                gb[HY + y, HZ : HZ + PL, cols] * (1.0 / NV)
-            )
         outs.append(pltpu.make_async_copy(est_v.at[c], out_ref.at[:, cols], lsem.at[NV + c]))
         outs[-1].start()
     for copy in outs:
@@ -382,7 +405,7 @@
         def _():
             for part in range(3):
                 z_copy(side, part).wait_send()
-            zb_copy(side).wait_send()
+                zb_copy(side, part).wait_send()
 
     for v in range(NV):
         pltpu.make_async_copy(
@@ -414,10 +437,9 @@
             pltpu.VMEM((NV, W, W), BF16),
             pltpu.VMEM((rows, W), BF16),
             pltpu.VMEM((rows, W), BF16),
-            pltpu.VMEM((RE, 2 * NV * PL, W), BF16),
+            pltpu.VMEM((RE, 3 * PL, W), BF16),
             pltpu.VMEM((NV * PL, 3 * PE), BF16),
-            pltpu.VMEM((PE, 2 * NV * PL), BF16),
-            pltpu.VMEM((PE, NV * PL), BF16),
+            pltpu.VMEM((NV, PE, 3 * PL), BF16),
             pltpu.VMEM((RE, PE, W), F32),
             pltpu.VMEM((2, RE, HZ, W), F32),
             pltpu.VMEM((2, HY, PL, W), F32),
@@ -428,8 +450,8 @@
             dma((2,)),
             dma((2, 3)),
             dma((2, 3)),
-            dma((2,)),
-            dma((2,)),
+            dma((2, 3)),
+            dma((2, 3)),
             dma((2,)),
             dma((2,)),
         ],

time: 113 us -> 107 us (0.947)
  Pallas kernels: 111 us -> 105 us
    pallas_call x1, Pallas kernels: 111 us -> 105 us  [local(): pl.pallas_call(kernel, out_shape=jax.ShapeDtypeStruct((rows, W), F32), in...]
where the time goes in v2:
time: 107 us
  Pallas kernels  105 us (98%)
  local copies, waits for them, and re-layouts  2.31 us (2%)
    pallas_call x1, Pallas kernels, local(): pl.pallas_call(kernel, out_shape=jax.ShapeDtypeStruct((rows, W), F32), in...  105 us
    unnamed x1, local copies, waits for them, and re-layouts  2.31 us

profile of v2, /device:TPU:33, one launch (start us, length us, event | category | flops | bytes accessed | tf_op | source)
XLA Modules:
  0.0 106.9 jit_solution(16081611605634807297)
XLA Ops:
  0.0 104.5 %shard_map.55 = f32[512,512]{1,0:T(8,128)} custom-call(f32[512,512]{1,0:T(8,128)} %bitcast.5, f32[4,512,512]{2,1,0:T(8,128)} %bitcast.3, s32[4,32]{1,0:T(4,128)} %order.1, f32[4,2,9]{2,1,0:T(2,128)} %lat.1, f32[4,33]{1,0:T(4,128)} %axial.1), custom_call_target="tpu_custom_call" | custom-call | tf_op jit(solution)/shard_map/pallas_call | solution.py:421
  104.6 2.3 %copy.7 = f32[32,16,512]{2,1,0:T(8,128)} copy(f32[32,16,512]{2,1,0:T(8,128)} %bitcast.4) | data formatting | bytes 2097152

commit v3 on v2

--- a/solution.py
+++ b/solution.py
@@ -63,8 +63,9 @@
 
 def kernel(
     est_hbm, obs_hbm, order, lat, axial, out_ref,
-    est_v, obs_v, snd, rcv, ext, axb, lh, ll, bl, qh, ql, rh, rl, tt, acat, adj, gb, zr, yr,
+    est_v, obs_v, snd, rcv, ext, axb, lh, ll, bl, qh, ql, rh, rl, tt, acat, adj, gb, zr, yr, dr,
     lsem, a_send, a_recv, y_send, y_recv, z_send, z_recv, zb_send, zb_recv, yb_send, yb_recv,
+    d_send, d_recv, db_send, db_recv,
 ):
     gy = lax.axis_index("gy")
     gz = lax.axis_index("gz")
@@ -91,6 +92,15 @@
     for other in (up_z, dn_z):
         pl.semaphore_signal(bar, inc=1, device_id=(gy, other), device_id_type=MESH)
 
+    middle = gz * (SLABS - 1 - gz) // 2
+
+    @pl.when(middle == 1)
+    def _():
+        for other in (up_y, dn_y):
+            pl.semaphore_signal(
+                bar, inc=1, device_id=(other, SLABS - 1 - gz), device_id_type=MESH
+            )
+
     for c, copy in enumerate(est_in):
         copy.wait()
         for y in range(RW):
@@ -112,7 +122,14 @@
     def _():
         ext[:, HZ + PL : PE, :] = jnp.zeros((RE, HZ, W), F32)
 
-    pl.semaphore_wait(bar, PEERS - 1 + 2)
+    for z_edge, planes in ((1, slice(HZ + PL, PE)), (2, slice(0, HZ))):
+        for y_edge, rows in ((0, slice(0, HY)), (PEERS - 1, slice(HY + RW, RE))):
+
+            @pl.when((gz == z_edge) & (gy == y_edge))
+            def _():
+                ext[rows, planes, :] = jnp.zeros((HY, HZ, W), F32)
+
+    pl.semaphore_wait(bar, PEERS - 1 + 2 + 2 * middle)
 
     def y_copy(side):
         src = (slice(HY, 2 * HY), slice(RW, RW + HY))[side]
@@ -131,6 +148,18 @@
             device_id=(gy, (dn_z, up_z)[side]), device_id_type=MESH,
         )
 
+    def d_copy(zs, ys):
+        rows = (slice(HY, 2 * HY), slice(RW, RW + HY))[ys]
+        to_rows = (slice(HY + RW, RE), slice(0, HY))[ys]
+        src = (slice(HZ, 2 * HZ), slice(PL, PL + HZ))[zs]
+        dst = (slice(HZ + PL, PE), slice(0, HZ))[zs]
+        return pltpu.make_async_remote_copy(
+            ext.at[rows, src], ext.at[to_rows, dst], d_send.at[zs, ys], d_recv.at[zs, ys],
+            device_id=((dn_y, up_y)[ys], (dn_z, up_z)[zs]), device_id_type=MESH,
+        )
+
+    on_chip = (gz % 2 == 1, gz % 2 == 0)
+    across = (gz == 2, gz == 1)
     has_y = (gy > 0, gy < PEERS - 1)
     has_z = (gz > 0, gz < SLABS - 1)
     for side in range(2):
@@ -143,6 +172,13 @@
         def _():
             z_copy(side, 0).start()
 
+    for zs in range(2):
+        for ys in range(2):
+
+            @pl.when(across[zs] & has_y[ys])
+            def _():
+                d_copy(zs, ys).start()
+
     def send_margins():
         for side in range(2):
 
@@ -152,7 +188,7 @@
 
         for side in range(2):
 
-            @pl.when(has_z[side])
+            @pl.when(on_chip[side])
             def _():
                 z_copy(side, 1).start()
                 z_copy(side, 2).start()
@@ -216,8 +252,18 @@
 
         @pl.when(has_z[1 - side])
         def _():
-            for part in range(3):
-                z_copy(side, part).wait_recv()
+            z_copy(side, 0).wait_recv()
+
+        @pl.when(on_chip[1 - side])
+        def _():
+            z_copy(side, 1).wait_recv()
+            z_copy(side, 2).wait_recv()
+
+        for ys in range(2):
+
+            @pl.when(across[1 - side] & has_y[1 - ys])
+            def _():
+                d_copy(side, ys).wait_recv()
 
     def axial_row(y, carry):
         high, low = split(ext[y])
@@ -327,17 +373,25 @@
             device_id=(gy, (dn_z, up_z)[side]), device_id_type=MESH,
         )
 
+    def db_copy(zs, ys):
+        rows = (slice(0, HY), slice(HY + RW, RE))[ys]
+        src = (slice(0, HZ), slice(HZ + PL, PE))[zs]
+        return pltpu.make_async_remote_copy(
+            gb.at[rows, src], dr.at[zs, ys], db_send.at[zs, ys], db_recv.at[zs, ys],
+            device_id=((dn_y, up_y)[ys], (dn_z, up_z)[zs]), device_id_type=MESH,
+        )
+
     def zb_start(part):
         for side in range(2):
 
-            @pl.when(has_z[side])
+            @pl.when((has_z if part == 2 else on_chip)[side])
             def _():
                 zb_copy(side, part).start()
 
     def zb_add(part):
         for side in range(2):
 
-            @pl.when(has_z[1 - side])
+            @pl.when((has_z if part == 2 else on_chip)[1 - side])
             def _():
                 zb_copy(side, part).wait_recv()
                 at = (slice(PL, PL + HZ), slice(HZ, 2 * HZ))[side]
@@ -347,8 +401,13 @@
     for part in range(2):
         axial_back(NV - 1, False, *parts[part])
         zb_start(part)
-    axial_back(NV - 1, False, *parts[2])
-    zb_start(2)
+    for zs in range(2):
+        for ys in range(2):
+
+            @pl.when(across[zs] & has_y[ys])
+            def _():
+                db_copy(zs, ys).start()
+
     for part in range(2):
         zb_add(part)
 
@@ -365,6 +424,8 @@
         def _():
             yb_copy(side).start()
 
+    axial_back(NV - 1, False, *parts[2])
+    zb_start(2)
     zb_add(2)
 
     def finish(rows):
@@ -384,6 +445,16 @@
             base = (RW, HY)[side]
             for y in range(HY):
                 gb[base + y, HZ : HZ + PL] = gb[base + y, HZ : HZ + PL] + yr[side, y]
+
+        for zs in range(2):
+
+            @pl.when(across[1 - zs] & has_y[1 - side])
+            def _():
+                db_copy(zs, side).wait_recv()
+                base = (RW, HY)[side]
+                at = (slice(PL, PL + HZ), slice(HZ, 2 * HZ))[zs]
+                for y in range(HY):
+                    gb[base + y, at] = gb[base + y, at] + dr[zs, side, y]
 
     finish([*range(HY), *range(RW - HY, RW)])
     outs = []
@@ -403,9 +474,21 @@
 
         @pl.when(has_z[side])
         def _():
-            for part in range(3):
-                z_copy(side, part).wait_send()
+            z_copy(side, 0).wait_send()
+            zb_copy(side, 2).wait_send()
+
+        @pl.when(on_chip[side])
+        def _():
+            for part in range(2):
+                z_copy(side, 1 + part).wait_send()
                 zb_copy(side, part).wait_send()
+
+        for ys in range(2):
+
+            @pl.when(across[side] & has_y[ys])
+            def _():
+                d_copy(side, ys).wait_send()
+                db_copy(side, ys).wait_send()
 
     for v in range(NV):
         pltpu.make_async_copy(
@@ -443,6 +526,7 @@
             pltpu.VMEM((RE, PE, W), F32),
             pltpu.VMEM((2, RE, HZ, W), F32),
             pltpu.VMEM((2, HY, PL, W), F32),
+            pltpu.VMEM((2, 2, HY, HZ, W), F32),
             dma((NV + CC,)),
             dma((NV,)),
             dma((NV,)),
@@ -454,6 +538,10 @@
             dma((2, 3)),
             dma((2,)),
             dma((2,)),
+            dma((2, 2)),
+            dma((2, 2)),
+            dma((2, 2)),
+            dma((2, 2)),
         ],
         compiler_params=pltpu.CompilerParams(
             collective_id=0, has_side_effects=True, vmem_limit_bytes=60 << 20

time: 107 us -> 104 us (0.972)
  Pallas kernels: 105 us -> 101 us
    pallas_call x1, Pallas kernels: 105 us -> 101 us  [local(): pl.pallas_call(kernel, out_shape=jax.ShapeDtypeStruct((rows, W), F32), in...]
where the time goes in v3:
time: 104 us; the launch traced here: 103 us
  Pallas kernels  101 us (97%)
  local copies, waits for them, and re-layouts  2.31 us (2%)
    pallas_call x1, Pallas kernels, local(): pl.pallas_call(kernel, out_shape=jax.ShapeDtypeStruct((rows, W), F32), in...  101 us
    unnamed x1, local copies, waits for them, and re-layouts  2.31 us

profile of v3, /device:TPU:33, one launch (start us, length us, event | category | flops | bytes accessed | tf_op | source)
XLA Modules:
  0.0 103.2 jit_solution(311691053731932679)
XLA Ops:
  0.0 100.8 %shard_map.55 = f32[512,512]{1,0:T(8,128)} custom-call(f32[512,512]{1,0:T(8,128)} %bitcast.5, f32[4,512,512]{2,1,0:T(8,128)} %bitcast.3, s32[4,32]{1,0:T(4,128)} %order.1, f32[4,2,9]{2,1,0:T(2,128)} %lat.1, f32[4,33]{1,0:T(4,128)} %axial.1), custom_call_target="tpu_custom_call" | custom-call | tf_op jit(solution)/shard_map/pallas_call | solution.py:504
  100.9 2.3 %copy.7 = f32[32,16,512]{2,1,0:T(8,128)} copy(f32[32,16,512]{2,1,0:T(8,128)} %bitcast.4) | data formatting | bytes 2097152

commit v4 on v3

--- a/solution.py
+++ b/solution.py
@@ -33,6 +33,12 @@
 ORDER = ((0, 0, 1),) + tuple((dz, dy, dx) for dz, dy in PLANE for dx in (1, 0))
 
 
+KEPT = (0, 1, 2, 3, 12, 13, 14, 15, 8, 9, 10, 11, 4, 5, 6, 7)
+PLACE = tuple(KEPT.index(y) for y in range(RW))
+EDGE = (*range(HY), *range(HY + RW, RE))
+INNER = tuple(range(HY, HY + RW))
+
+
 def split(value):
     high = value.astype(BF16)
     return high, (value - high.astype(F32)).astype(BF16)
@@ -193,26 +199,39 @@
                 z_copy(side, 1).start()
                 z_copy(side, 2).start()
 
+    upper = lax.broadcasted_iota(jnp.int32, (8, 128), 0) < HY
+
+    def parts_of(v, ref, at):
+        if isinstance(v, int) and v == NV - 1:
+            return [(ref.at[v, at, :, h * 8 : (h + 1) * 8], v + h) for h in range(2)]
+        return [(ref.at[v, at], v)]
+
     def send_view(v, carry):
         pltpu.make_async_copy(obs_hbm.at[v], obs_v.at[v], lsem.at[v]).wait()
         for g in range(ZG):
             for c in range(4):
                 t = obs_v[v, g * 128 : (g + 1) * 128, c * 128 : (c + 1) * 128].T
                 for d in range(8):
-                    snd[v, c * 8 + d, g] = t[d * RW : (d + 1) * RW, :]
+                    first = t[d * RW : d * RW + 8, :]
+                    second = t[d * RW + 8 : (d + 1) * RW, :]
+                    snd[v, c * 8 + d, g, 0:8] = jnp.where(upper, first, second)
+                    snd[v, c * 8 + d, g, 8:RW] = jnp.where(upper, second, first)
         rcv[v, gy] = snd[v, gy]
 
-        for offset in ORDER:
-            to = peer(*offset)
-            pltpu.make_async_remote_copy(
-                snd.at[v, to], rcv.at[v, gy], a_send.at[v], a_recv.at[v],
-                device_id=(to, gz), device_id_type=MESH,
-            ).start()
+        for h in range(len(parts_of(v, snd, 0))):
+            for offset in ORDER:
+                to = peer(*offset)
+                src, n = parts_of(v, snd, to)[h]
+                dst, _ = parts_of(v, rcv, gy)[h]
+                pltpu.make_async_remote_copy(
+                    src, dst, a_send.at[n], a_recv.at[n], device_id=(to, gz), device_id_type=MESH
+                ).start()
         return carry
 
     send_view(0, 0)
     send_margins()
-    lax.fori_loop(1, NV, send_view, 0)
+    lax.fori_loop(1, NV - 1, send_view, 0)
+    send_view(NV - 1, 0)
 
     i0 = lax.broadcasted_iota(jnp.int32, (PL, PE), 0)
     i1 = lax.broadcasted_iota(jnp.int32, (PL, PE), 1)
@@ -285,8 +304,8 @@
                 for j in range(1, TLAT):
                     acc = acc + taps[j] * rows[y + j]
                 high, low = split(acc)
-                lh[v, pl.ds(y * PL + m, 16), cols] = high
-                ll[v, pl.ds(y * PL + m, 16), cols] = low
+                lh[v, pl.ds(PLACE[y] * PL + m, 16), cols] = high
+                ll[v, pl.ds(PLACE[y] * PL + m, 16), cols] = low
         return carry
 
     lax.fori_loop(0, NV * 2, row_tile, 0)
@@ -301,36 +320,57 @@
 
     lax.fori_loop(0, NV, col_view, 0)
 
-    def back_view(v):
-        pltpu.make_async_copy(
-            rcv.at[v, pl.ds(0, PEERS - 1)], rcv.at[v, pl.ds(0, PEERS - 1)], a_recv.at[v]
-        ).wait()
-
+    def arrived(v):
+        for h in range(len(parts_of(v, rcv, 0))):
+            yield lambda h=h: pltpu.make_async_copy(
+                parts_of(v, rcv, pl.ds(0, PEERS - 1))[h][0],
+                parts_of(v, rcv, pl.ds(0, PEERS - 1))[h][0],
+                a_recv.at[parts_of(v, rcv, 0)[h][1]],
+            ).wait()
+
+    def ratio(v, halves):
         def group(g, inner):
-            for s in range(PEERS // 8):
-                cols = slice(s * 128, (s + 1) * 128)
-                vals = swap_chunks([rcv[v, s * 8 + k, g] for k in range(8)], RW)
-                for z in range(8):
-                    den = bl[v, s, pl.ds(g * 8 + z, RW, stride=PL), :]
-                    high, low = split(vals[z] / den)
-                    at = pl.multiple_of(g * 128 + z * 16, 16)
-                    rh[pl.ds(at, 16), cols] = high
-                    rl[pl.ds(at, 16), cols] = low
+            for h in halves:
+                for s in range(PEERS // 8):
+                    cols = slice(s * 128, (s + 1) * 128)
+                    vals = swap_chunks(
+                        [rcv[v, s * 8 + k, g, h * 8 : (h + 1) * 8] for k in range(8)], RW
+                    )
+                    vals = [
+                        vals[z] / bl[v, s, pl.ds(h * 256 + g * 8 + z, 8, stride=PL), :]
+                        for z in range(8)
+                    ]
+                    for z in range(0, 8, 2):
+                        high, low = split(jnp.concatenate(vals[z : z + 2], axis=0))
+                        at = pl.multiple_of(h * 256 + g * 64 + z * 8, 16)
+                        rh[pl.ds(at, 16), cols] = high
+                        rl[pl.ds(at, 16), cols] = low
             return inner
 
         lax.fori_loop(0, ZG, group, 0)
+
+    def columns_back(v, start, stop):
+        at = slice(start, stop)
         for n in range(2):
             rows = slice(n * 256, (n + 1) * 256)
-            res = dot_nt(rh[...], qh[v, rows, :]) + dot_nt(rl[...], qh[v, rows, :]) + dot_nt(rh[...], ql[v, rows, :])
-            bl[v, 2 * n] = res[:, :128]
-            bl[v, 2 * n + 1] = res[:, 128:]
+            res = (
+                dot_nt(rh[at], qh[v, rows, :]) + dot_nt(rl[at], qh[v, rows, :]) + dot_nt(rh[at], ql[v, rows, :])
+            )
+            bl[v, 2 * n, at] = res[:, :128]
+            bl[v, 2 * n + 1, at] = res[:, 128:]
+
+    def rows_back(v, outs):
         taps = [lat[v, 0, j] for j in range(TLAT)]
+        used = sorted({y - j for y in outs for j in range(TLAT) if 0 <= y - j < RW})
 
         def spread(h, inner):
             for c in range(W // 128):
                 cols = slice(c * 128, (c + 1) * 128)
-                rows = [bl[v, c, pl.ds(h * 256 + y, 16, stride=RW), :] for y in range(RW)]
-                for y in range(RE):
+                rows = {
+                    y: bl[v, c, pl.ds(PLACE[y] // 8 * 256 + h * 128 + PLACE[y] % 8, 16, stride=8), :]
+                    for y in used
+                }
+                for y in outs:
                     acc = None
                     for j in range(TLAT):
                         if 0 <= y - j < RW:
@@ -353,15 +393,27 @@
 
         lax.fori_loop(start, stop, row, 0, unroll=4)
 
-    def whole_view(v, carry):
-        back_view(v)
-        axial_back(v, False, 0, RE)
+    def whole_view(v, first):
+        for wait in arrived(v):
+            wait()
+        ratio(v, (0, 1))
+        columns_back(v, 0, 512)
+        rows_back(v, range(RE))
+        axial_back(v, first, 0, RE)
+
+    def next_view(v, carry):
+        whole_view(v, False)
         return carry
 
-    back_view(0)
-    axial_back(0, True, 0, RE)
-    lax.fori_loop(1, NV - 1, whole_view, 0)
-    back_view(NV - 1)
+    whole_view(0, True)
+    lax.fori_loop(1, NV - 1, next_view, 0)
+
+    last = NV - 1
+    edge_in, inner_in = arrived(last)
+    edge_in()
+    ratio(last, (0,))
+    columns_back(last, 0, 256)
+    rows_back(last, EDGE)
 
     parts = ((0, HY), (HY + RW, RE), (HY, HY + RW))
 
@@ -399,7 +451,7 @@
                     gb[y, at] = gb[y, at] + zr[side, y]
 
     for part in range(2):
-        axial_back(NV - 1, False, *parts[part])
+        axial_back(last, False, *parts[part])
         zb_start(part)
     for zs in range(2):
         for ys in range(2):
@@ -424,7 +476,11 @@
         def _():
             yb_copy(side).start()
 
-    axial_back(NV - 1, False, *parts[2])
+    inner_in()
+    ratio(last, (1,))
+    columns_back(last, 256, 512)
+    rows_back(last, INNER)
+    axial_back(last, False, *parts[2])
     zb_start(2)
     zb_add(2)
 
@@ -491,9 +547,8 @@
                 db_copy(side, ys).wait_send()
 
     for v in range(NV):
-        pltpu.make_async_copy(
-            snd.at[v, pl.ds(0, PEERS - 1)], snd.at[v, pl.ds(0, PEERS - 1)], a_send.at[v]
-        ).wait()
+        for block, n in parts_of(v, snd, pl.ds(0, PEERS - 1)):
+            pltpu.make_async_copy(block, block, a_send.at[n]).wait()
 
 
 def local(estimate, observed, tile_order, lateral_taps, axial_taps):
@@ -528,8 +583,8 @@
             pltpu.VMEM((2, HY, PL, W), F32),
             pltpu.VMEM((2, 2, HY, HZ, W), F32),
             dma((NV + CC,)),
-            dma((NV,)),
-            dma((NV,)),
+            dma((NV + 1,)),
+            dma((NV + 1,)),
             dma((2,)),
             dma((2,)),
             dma((2, 3)),

time: 104 us -> 102 us (0.981)
  Pallas kernels: 101 us -> 98.3 us
    pallas_call x1, Pallas kernels: 101 us -> 98.3 us  [local(): pl.pallas_call(kernel, out_shape=jax.ShapeDtypeStruct((rows, W), F32), in...]
where the time goes in v4:
time: 102 us; the launch traced here: 101 us
  Pallas kernels  98.3 us (96%)
  local copies, waits for them, and re-layouts  2.31 us (2%)
    pallas_call x1, Pallas kernels, local(): pl.pallas_call(kernel, out_shape=jax.ShapeDtypeStruct((rows, W), F32), in...  98.3 us
    unnamed x1, local copies, waits for them, and re-layouts  2.31 us

profile of v4, /device:TPU:33, one launch (start us, length us, event | category | flops | bytes accessed | tf_op | source)
XLA Modules:
  0.0 100.6 jit_solution(1488443030561074054)
XLA Ops:
  0.0 98.3 %shard_map.55 = f32[512,512]{1,0:T(8,128)} custom-call(f32[512,512]{1,0:T(8,128)} %bitcast.5, f32[4,512,512]{2,1,0:T(8,128)} %bitcast.3, s32[4,32]{1,0:T(4,128)} %order.1, f32[4,2,9]{2,1,0:T(2,128)} %lat.1, f32[4,33]{1,0:T(4,128)} %axial.1), custom_call_target="tpu_custom_call" | custom-call | tf_op jit(solution)/shard_map/pallas_call | solution.py:559
  98.3 2.3 %copy.7 = f32[32,16,512]{2,1,0:T(8,128)} copy(f32[32,16,512]{2,1,0:T(8,128)} %bitcast.4) | data formatting | bytes 2097152

commit v5 on v4

--- a/solution.py
+++ b/solution.py
@@ -30,7 +30,12 @@
 PLANE = (
     (1, 0), (0, 1), (3, 0), (0, 3), (2, 1), (1, 2), (2, 3), (3, 2), (1, 1), (3, 3), (1, 3), (3, 1), (2, 0), (0, 2), (2, 2),
 )
-ORDER = ((0, 0, 1),) + tuple((dz, dy, dx) for dz, dy in PLANE for dx in (1, 0))
+ORDER = tuple(
+    sorted(
+        ((0, 0, 1),) + tuple((dz, dy, dx) for dz, dy in PLANE for dx in (1, 0)),
+        key=lambda o: -(min(o[0], 4 - o[0]) + min(o[1], 4 - o[1]) + o[2]),
+    )
+)
 
 
 KEPT = (0, 1, 2, 3, 12, 13, 14, 15, 8, 9, 10, 11, 4, 5, 6, 7)
@@ -168,22 +173,38 @@
     across = (gz == 2, gz == 1)
     has_y = (gy > 0, gy < PEERS - 1)
     has_z = (gz > 0, gz < SLABS - 1)
-    for side in range(2):
+    def y_piece(side, p):
+        src = (HY, RW)[side]
+        dst = (HY + RW, 0)[side]
+        at = slice(HZ + p * 8, HZ + p * 8 + 8)
 
         @pl.when(has_y[side])
         def _():
-            y_copy(side).start()
+            pltpu.make_async_remote_copy(
+                ext.at[src : src + HY, at], ext.at[dst : dst + HY, at], y_send.at[side], y_recv.at[side],
+                device_id=((dn_y, up_y)[side], gz), device_id_type=MESH,
+            ).start()
+
+    def z_piece(side, p):
+        rows = slice(HY + 4 * p, HY + 4 * p + 4)
+        src = (slice(HZ, 2 * HZ), slice(PL, PL + HZ))[side]
+        dst = (slice(HZ + PL, PE), slice(0, HZ))[side]
 
         @pl.when(has_z[side])
         def _():
-            z_copy(side, 0).start()
-
-    for zs in range(2):
-        for ys in range(2):
-
-            @pl.when(across[zs] & has_y[ys])
-            def _():
-                d_copy(zs, ys).start()
+            pltpu.make_async_remote_copy(
+                ext.at[rows, src], ext.at[rows, dst], z_send.at[side, 0], z_recv.at[side, 0],
+                device_id=(gy, (dn_z, up_z)[side]), device_id_type=MESH,
+            ).start()
+
+    def d_piece(zs, ys):
+        @pl.when(across[zs] & has_y[ys])
+        def _():
+            d_copy(zs, ys).start()
+
+    y_pieces = [functools.partial(y_piece, side, p) for p in range(4) for side in range(2)]
+    z_pieces = [functools.partial(z_piece, side, p) for p in range(4) for side in range(2)]
+    z_pieces += [functools.partial(d_piece, a, b) for a in range(2) for b in range(2)]
 
     def send_margins():
         for side in range(2):
@@ -206,7 +227,8 @@
             return [(ref.at[v, at, :, h * 8 : (h + 1) * 8], v + h) for h in range(2)]
         return [(ref.at[v, at], v)]
 
-    def send_view(v, carry):
+    def send_view(v, carry, between=()):
+        between = list(between)
         pltpu.make_async_copy(obs_hbm.at[v], obs_v.at[v], lsem.at[v]).wait()
         for g in range(ZG):
             for c in range(4):
@@ -220,6 +242,8 @@
 
         for h in range(len(parts_of(v, snd, 0))):
             for offset in ORDER:
+                if between:
+                    between.pop(0)()
                 to = peer(*offset)
                 src, n = parts_of(v, snd, to)[h]
                 dst, _ = parts_of(v, rcv, gy)[h]
@@ -228,9 +252,10 @@
                 ).start()
         return carry
 
-    send_view(0, 0)
+    send_view(0, 0, y_pieces + z_pieces)
+    send_view(1, 0)
     send_margins()
-    lax.fori_loop(1, NV - 1, send_view, 0)
+    lax.fori_loop(2, NV - 1, send_view, 0)
     send_view(NV - 1, 0)
 
     i0 = lax.broadcasted_iota(jnp.int32, (PL, PE), 0)

time: 102 us -> 98.8 us (0.969)
  Pallas kernels: 98.3 us -> 95.9 us
    pallas_call x1, Pallas kernels: 98.3 us -> 95.9 us  [local(): pl.pallas_call(kernel, out_shape=jax.ShapeDtypeStruct((rows, W), F32), in...]
where the time goes in v5:
time: 98.8 us; the launch traced here: 98.2 us
  Pallas kernels  95.9 us (97%)
  local copies, waits for them, and re-layouts  2.31 us (2%)
    pallas_call x1, Pallas kernels, local(): pl.pallas_call(kernel, out_shape=jax.ShapeDtypeStruct((rows, W), F32), in...  95.9 us
    unnamed x1, local copies, waits for them, and re-layouts  2.31 us

profile of v5, /device:TPU:33, one launch (start us, length us, event | category | flops | bytes accessed | tf_op | source)
XLA Modules:
  0.0 98.2 jit_solution(9701371908331249041)
XLA Ops:
  0.0 95.9 %shard_map.55 = f32[512,512]{1,0:T(8,128)} custom-call(f32[512,512]{1,0:T(8,128)} %bitcast.5, f32[4,512,512]{2,1,0:T(8,128)} %bitcast.3, s32[4,32]{1,0:T(4,128)} %order.1, f32[4,2,9]{2,1,0:T(2,128)} %lat.1, f32[4,33]{1,0:T(4,128)} %axial.1), custom_call_target="tpu_custom_call" | custom-call | tf_op jit(solution)/shard_map/pallas_call | solution.py:584
  95.9 2.3 %copy.7 = f32[32,16,512]{2,1,0:T(8,128)} copy(f32[32,16,512]{2,1,0:T(8,128)} %bitcast.4) | data formatting | bytes 2097152

commit v6 on v5

--- a/solution.py
+++ b/solution.py
@@ -91,8 +91,10 @@
     for v in range(NV):
         pltpu.make_async_copy(obs_hbm.at[v], obs_v.at[v], lsem.at[v]).start()
 
+    way = 1 - 2 * (gz % 2)
+
     def peer(dz, dy, dx):
-        return ((cz + dz) % 4) * 8 + ((cy + dy) % 4) * 2 + (cx + dx) % 2
+        return ((cz + 4 + way * dz) % 4) * 8 + ((cy + 4 + way * dy) % 4) * 2 + (cx + dx) % 2
 
     bar = pltpu.get_barrier_semaphore()
 
@@ -252,7 +254,9 @@
                 ).start()
         return carry
 
-    send_view(0, 0, y_pieces + z_pieces)
+    for piece in y_pieces[:4]:
+        piece()
+    send_view(0, 0, y_pieces[4:] + z_pieces)
     send_view(1, 0)
     send_margins()
     lax.fori_loop(2, NV - 1, send_view, 0)

time: 98.8 us -> 98.6 us (level)
  no operation moved by 1% of the time
where the time goes in v6:
time: 98.6 us; the launch traced here: 97.9 us
  Pallas kernels  95.6 us (97%)
  local copies, waits for them, and re-layouts  2.31 us (2%)
    pallas_call x1, Pallas kernels, local(): pl.pallas_call(kernel, out_shape=jax.ShapeDtypeStruct((rows, W), F32), in...  95.6 us
    unnamed x1, local copies, waits for them, and re-layouts  2.31 us

profile of v6, /device:TPU:33, one launch (start us, length us, event | category | flops | bytes accessed | tf_op | source)
XLA Modules:
  0.0 97.9 jit_solution(3865084874523410989)
XLA Ops:
  0.0 95.6 %shard_map.55 = f32[512,512]{1,0:T(8,128)} custom-call(f32[512,512]{1,0:T(8,128)} %bitcast.5, f32[4,512,512]{2,1,0:T(8,128)} %bitcast.3, s32[4,32]{1,0:T(4,128)} %order.1, f32[4,2,9]{2,1,0:T(2,128)} %lat.1, f32[4,33]{1,0:T(4,128)} %axial.1), custom_call_target="tpu_custom_call" | custom-call | tf_op jit(solution)/shard_map/pallas_call | solution.py:588
  95.6 2.3 %copy.7 = f32[32,16,512]{2,1,0:T(8,128)} copy(f32[32,16,512]{2,1,0:T(8,128)} %bitcast.4) | data formatting | bytes 2097152

commit v7 on v5

--- a/solution.py
+++ b/solution.py
@@ -509,8 +509,8 @@
     zb_start(2)
     zb_add(2)
 
-    def finish(rows):
-        for c in range(CC):
+    def finish(rows, chunks=range(CC)):
+        for c in chunks:
             cols = slice(c * 128, (c + 1) * 128)
             for y in rows:
                 est_v[c, pl.ds(y, PL, stride=RW), :] = ext[HY + y, HZ : HZ + PL, cols] * (
@@ -537,14 +537,12 @@
                 for y in range(HY):
                     gb[base + y, at] = gb[base + y, at] + dr[zs, side, y]
 
-    finish([*range(HY), *range(RW - HY, RW)])
     outs = []
     for c in range(CC):
+        finish([*range(HY), *range(RW - HY, RW)], [c])
         cols = slice(c * 128, (c + 1) * 128)
         outs.append(pltpu.make_async_copy(est_v.at[c], out_ref.at[:, cols], lsem.at[NV + c]))
         outs[-1].start()
-    for copy in outs:
-        copy.wait()
 
     for side in range(2):
 
@@ -574,6 +572,8 @@
     for v in range(NV):
         for block, n in parts_of(v, snd, pl.ds(0, PEERS - 1)):
             pltpu.make_async_copy(block, block, a_send.at[n]).wait()
+    for copy in outs:
+        copy.wait()
 
 
 def local(estimate, observed, tile_order, lateral_taps, axial_taps):

time: 98.8 us -> 98.6 us (level)
  no operation moved by 1% of the time
where the time goes in v7:
time: 98.6 us; the launch traced here: 98 us
  Pallas kernels  95.7 us (97%)
  local copies, waits for them, and re-layouts  2.31 us (2%)
    pallas_call x1, Pallas kernels, local(): pl.pallas_call(kernel, out_shape=jax.ShapeDtypeStruct((rows, W), F32), in...  95.7 us
    unnamed x1, local copies, waits for them, and re-layouts  2.31 us

profile of v7, /device:TPU:33, one launch (start us, length us, event | category | flops | bytes accessed | tf_op | source)
XLA Modules:
  0.0 98.0 jit_solution(15482574643582393060)
XLA Ops:
  0.0 95.7 %shard_map.55 = f32[512,512]{1,0:T(8,128)} custom-call(f32[512,512]{1,0:T(8,128)} %bitcast.5, f32[4,512,512]{2,1,0:T(8,128)} %bitcast.3, s32[4,32]{1,0:T(4,128)} %order.1, f32[4,2,9]{2,1,0:T(2,128)} %lat.1, f32[4,33]{1,0:T(4,128)} %axial.1), custom_call_target="tpu_custom_call" | custom-call | tf_op jit(solution)/shard_map/pallas_call | solution.py:584
  95.7 2.3 %copy.7 = f32[32,16,512]{2,1,0:T(8,128)} copy(f32[32,16,512]{2,1,0:T(8,128)} %bitcast.4) | data formatting | bytes 2097152
